TPU v7x, 128 devices: a whole 4x4x4 slice. The times are simulated.
128 devices in a mesh: fsdp: 32 (over x, z, core), ckpt: 4 (over y).
Axes of the slice: x: 4, y: 4, z: 4, core: 2. Of those that a mesh axis runs over, the one named last changes fastest.
Arguments:
- act_table: bfloat16 [4, 2048, 4096], P('ckpt', 'fsdp'), may hold values from -6 to 6
- token_ids: int32 [4, 2048], P('ckpt'), may hold values from 0 to 2047, each once within a row
- lengths: int32 [4, 8], P('ckpt'), may hold values from 1 to 384, 2048 in all within a row
- grads: bfloat16 [4, 2048, 14336], P('ckpt', 'fsdp'), may hold values from -0.19921875 to 0.19921875
- weights: bfloat16 [4, 32, 1024, 1792], P('ckpt', 'fsdp'), may hold values from -6 to 6
Outputs:
- merged: bfloat16 [32, 1024, 1792], P('fsdp', 'ckpt')
- merge_weight: float32 [32, 1024, 1792], P('fsdp', 'ckpt')
Inputs may be any that keep to these rules, and one draw needn't show every extreme that they name: `token_ids`: each checkpoint's row names every row of the activation table once. One checkpoint's lengths sum to 2048, and one of them is exactly 384.
All inputs are finite; a program needn't handle non-finite values.
Results may differ from a plain program's by a relative error of at most 0.001.
Values may be sent and summed in bfloat16 or wider, within the bound.
A program may use at most 128 MiB of HBM per device.

v0:
```python
import jax
import jax.numpy as jnp
from jax import lax
from jax.sharding import PartitionSpec as P

NCB = 8
MOST = 384


prior_mass = 0.1


def example_fisher(act_rows, grad_rows, example_lengths, longest):
    row_starts = jnp.cumsum(example_lengths) - example_lengths
    padded_rows = jnp.concatenate(
        [act_rows, jnp.zeros((longest, act_rows.shape[1]), act_rows.dtype)], 0
    )
    padded_grads = jnp.concatenate(
        [grad_rows, jnp.zeros((longest, grad_rows.shape[1]), grad_rows.dtype)], 0
    )
    positions = jnp.arange(longest, dtype=jnp.int32)

    def add_example(example, running):
        row_start = row_starts[example]
        act_block = lax.dynamic_slice_in_dim(padded_rows, row_start, longest, 0)
        keep = (positions < example_lengths[example])[:, None]
        act_block = jnp.where(keep, act_block, jnp.zeros_like(act_block))
        grad_block = lax.dynamic_slice_in_dim(padded_grads, row_start, longest, 0)
        example_grad = lax.dot_general(
            act_block, grad_block, (((0,), (0,)), ((), ())), preferred_element_type=jnp.float32
        )
        return running + example_grad * example_grad

    start_value = jnp.zeros((act_rows.shape[1], grad_rows.shape[1]), jnp.float32)
    return lax.fori_loop(0, example_lengths.shape[0], add_example, start_value)


def body(act_table, token_ids, lengths, grads, weights):
    group_width = lax.axis_size("fsdp")
    row_blocks = group_width // NCB
    own_rows = act_table[0]
    local_count = own_rows.shape[0]
    feature_width = own_rows.shape[1] // row_blocks
    act_parts = jnp.broadcast_to(
        own_rows.reshape(local_count, row_blocks, 1, feature_width),
        (local_count, row_blocks, NCB, feature_width),
    )
    act_parts = act_parts.reshape(local_count, group_width * feature_width)
    table_rows = lax.all_to_all(act_parts, "fsdp", split_axis=1, concat_axis=0, tiled=True)
    act_rows = table_rows[token_ids[0]]
    own_grads = grads[0]
    grad_width = own_grads.shape[1]
    grad_parts = jnp.broadcast_to(
        own_grads.reshape(local_count, 1, grad_width), (local_count, row_blocks, grad_width)
    )
    grad_parts = grad_parts.reshape(local_count, row_blocks * grad_width)
    grad_rows = lax.all_to_all(grad_parts, "fsdp", split_axis=1, concat_axis=0, tiled=True)
    fisher = example_fisher(act_rows, grad_rows, lengths[0], MOST)
    fisher_mass = fisher + prior_mass
    own_weight = weights[0, 0]
    group_size = lax.axis_size("ckpt")
    numerator, denominator = (
        lax.psum_scatter(
            fisher_mass * own_weight.astype(jnp.float32), "ckpt", scatter_dimension=0, tiled=True
        ),
        lax.psum_scatter(fisher_mass, "ckpt", scatter_dimension=0, tiled=True),
    )
    return ((numerator / denominator).astype(jnp.bfloat16)[None], (denominator / group_size)[None])


def solution(mesh):
    placed = (
        P("ckpt", "fsdp", None),
        P("ckpt", None),
        P("ckpt", None),
        P("ckpt", "fsdp", None),
        P("ckpt", "fsdp", None, None),
    )
    return jax.shard_map(
        body,
        mesh=mesh,
        in_specs=placed,
        out_specs=(P("fsdp", "ckpt", None), P("fsdp", "ckpt", None)),
        check_vma=False,
    )
```

profile of v0, /device:TPU:1, one launch (start us, length us, event | category | flops | bytes accessed | tf_op | source)
XLA Modules:
  0.0 465.6 jit_solution(11593485093440058547)
XLA Ops:
  7.2 1.4 broadcast_in_dim.47
  8.8 2.5 broadcast_in_dim.48
  11.3 9.5 %all-to-all-start = ((bf16[64,32,1024]{2,0,1:T(8,128)(2,1)}), bf16[64,32,1024]{2,0,1:T(8,128)(2,1)}, u32[]{:S(2)}, u32[]{:S(2)}) async-start(bf16[64,32,1024]{2,0,1:T(8,128)(2,1)} %bitcast.29), calls=%async_computation | async-start | bytes 8388608 | tf_op jit(solution)/shard_map/all_to_all | solution.py:49
  20.8 6.1 %broadcast_in_dim.50 = bf16[64,4,14336]{2,1,0:T(4,128)(2,1)} broadcast(bf16[64,14336]{1,0:T(8,128)(2,1)S(1)} %bitcast.30), dimensions={0,2} | broadcast | bytes 9175040 | tf_op jit(solution)/shard_map/broadcast_in_dim | solution.py:53
  26.9 13.3 %all_to_all.32 = bf16[64,32,1792]{2,1,0:T(8,128)(2,1)} reshape(bf16[64,4,14336]{2,1,0:T(4,128)(2,1)} %broadcast_in_dim.50) | data formatting | bytes 14680064 | tf_op jit(solution)/shard_map/all_to_all | solution.py:57
  40.2 10.1 %copy.12 = bf16[64,32,1792]{2,0,1:T(8,128)(2,1)} copy(bf16[64,32,1792]{2,1,0:T(8,128)(2,1)} %all_to_all.32) | data formatting | bytes 14680064 | tf_op jit(solution)/shard_map/all_to_all | solution.py:57
  50.3 22.7 %all-to-all-done = bf16[64,32,1024]{2,0,1:T(8,128)(2,1)} async-done(((bf16[64,32,1024]{2,0,1:T(8,128)(2,1)}), bf16[64,32,1024]{2,0,1:T(8,128)(2,1)}, u32[]{:S(2)}, u32[]{:S(2)}) %all-to-all-start) | async-done | bytes 4194336 | tf_op jit(solution)/shard_map/all_to_all | solution.py:49
  73.0 7.2 %all-to-all-start.1 = ((bf16[64,32,1792]{2,0,1:T(8,128)(2,1)}), bf16[64,32,1792]{2,0,1:T(8,128)(2,1)}, u32[]{:S(2)}, u32[]{:S(2)}) async-start(bf16[64,32,1792]{2,0,1:T(8,128)(2,1)} %copy.12), calls=%async_computation.1 | async-start | bytes 14680064 | tf_op jit(solution)/shard_map/all_to_all | solution.py:57
  80.6 13.7 %gather_fusion = bf16[2048,1024]{1,0:T(8,128)(2,1)} fusion(bf16[2048,1024]{1,0:T(8,128)(2,1)} %bitcast.5, s32[2048]{0:T(1024)S(1)} %broadcast_clamp_fusion), kind=kCustom, calls=%fused_computation | custom fusion | bytes 8396800 | tf_op jit(solution)/shard_map/gather | solution.py:50
  94.3 5.0 %concatenate.6 = bf16[2432,1024]{1,0:T(8,128)(2,1)} pad(bf16[2048,1024]{1,0:T(8,128)(2,1)} %gather_fusion, bf16[]{:T(256)} %constant.49.clone.1), padding=0_384x0_0 | pad | bytes 9175042 | tf_op jit(solution)/shard_map/concatenate | solution.py:15
  99.4 71.9 %all-to-all-done.1 = bf16[64,32,1792]{2,0,1:T(8,128)(2,1)} async-done(((bf16[64,32,1792]{2,0,1:T(8,128)(2,1)}), bf16[64,32,1792]{2,0,1:T(8,128)(2,1)}, u32[]{:S(2)}, u32[]{:S(2)}) %all-to-all-start.1) | async-done | bytes 7340064 | tf_op jit(solution)/shard_map/all_to_all | solution.py:57
  171.3 7.0 %concatenate.7 = bf16[2432,1792]{1,0:T(8,128)(2,1)} pad(bf16[2048,1792]{1,0:T(8,128)(2,1)} %bitcast.10, bf16[]{:T(256)} %constant.49.clone.1), padding=0_384x0_0 | pad | bytes 16056322 | tf_op jit(solution)/shard_map/concatenate | solution.py:18
  178.3 100.5 %while.14 = (s32[]{:T(128)}, f32[1024,1792]{1,0:T(8,128)}, s32[8]{0:T(128)S(1)}, s32[8]{0:T(128)S(1)}, bf16[2432,1024]{1,0:T(8,128)(2,1)}, /*index=5*/bf16[2432,1792]{1,0:T(8,128)(2,1)}, s32[]{:T(128)}, s32[]{:T(128)}, s32[]{:T(128)}) while((s32[]{:T(128)}, f32[1024,1792]{1,0:T(8,128)}, s32[8]{0:T(128)S(1)}, s32[8]{0:T(128)S(1)}, ...), condition=%wide.region_2.3_spmd.clone, body=%wide.region_1.2_spmd.clone.sunk | while | flops 1415184768 | bytes 16845228 | solution.py:35
  178.3 0.6 dynamic_slice.45
  182.1 6.9 %select_add_fusion.2 = f32[1024,1792]{1,0:T(8,128)} fusion(f32[1024,1792]{1,0:T(8,128)} %get-tuple-element.213, pred[]{:T(512)S(6)} %compare.5, bf16[2432,1792]{1,0:T(8,128)(2,1)} %get-tuple-element.226, s32[]{:T(128)S(6)} %select_n.41, bf16[2432,1024]{1,0:T(8,128)(2,1)} %get-tuple-element.225, pred[384]{0:T(512)(128)(4,1)S(1)} %iota_compare_fusion.2), kind=kOutput, calls=%fused_computation.2.clone.1 | convolution fusion | flops 1415184384 | bytes 16844672 | tf_op jit(solution)/shard_map/while/body/eval_jaxpr/dot_general | solution.py:29
  189.0 0.6 dynamic_slice.45
  192.7 9.0 %select_add_fusion.2 = f32[1024,1792]{1,0:T(8,128)} fusion(f32[1024,1792]{1,0:T(8,128)} %get-tuple-element.213, pred[]{:T(512)S(6)} %compare.5, bf16[2432,1792]{1,0:T(8,128)(2,1)} %get-tuple-element.226, s32[]{:T(128)S(6)} %select_n.41, bf16[2432,1024]{1,0:T(8,128)(2,1)} %get-tuple-element.225, pred[384]{0:T(512)(128)(4,1)S(1)} %iota_compare_fusion.2), kind=kOutput, calls=%fused_computation.2.clone.1 | convolution fusion | flops 1415184384 | bytes 16844672 | tf_op jit(solution)/shard_map/while/body/eval_jaxpr/dot_general | solution.py:29
  201.8 0.6 dynamic_slice.45
  205.6 9.0 %select_add_fusion.2 = f32[1024,1792]{1,0:T(8,128)} fusion(f32[1024,1792]{1,0:T(8,128)} %get-tuple-element.213, pred[]{:T(512)S(6)} %compare.5, bf16[2432,1792]{1,0:T(8,128)(2,1)} %get-tuple-element.226, s32[]{:T(128)S(6)} %select_n.41, bf16[2432,1024]{1,0:T(8,128)(2,1)} %get-tuple-element.225, pred[384]{0:T(512)(128)(4,1)S(1)} %iota_compare_fusion.2), kind=kOutput, calls=%fused_computation.2.clone.1 | convolution fusion | flops 1415184384 | bytes 16844672 | tf_op jit(solution)/shard_map/while/body/eval_jaxpr/dot_general | solution.py:29
  214.6 0.6 dynamic_slice.45
  218.4 9.0 %select_add_fusion.2 = f32[1024,1792]{1,0:T(8,128)} fusion(f32[1024,1792]{1,0:T(8,128)} %get-tuple-element.213, pred[]{:T(512)S(6)} %compare.5, bf16[2432,1792]{1,0:T(8,128)(2,1)} %get-tuple-element.226, s32[]{:T(128)S(6)} %select_n.41, bf16[2432,1024]{1,0:T(8,128)(2,1)} %get-tuple-element.225, pred[384]{0:T(512)(128)(4,1)S(1)} %iota_compare_fusion.2), kind=kOutput, calls=%fused_computation.2.clone.1 | convolution fusion | flops 1415184384 | bytes 16844672 | tf_op jit(solution)/shard_map/while/body/eval_jaxpr/dot_general | solution.py:29
  227.5 0.6 dynamic_slice.45
  231.3 9.0 %select_add_fusion.2 = f32[1024,1792]{1,0:T(8,128)} fusion(f32[1024,1792]{1,0:T(8,128)} %get-tuple-element.213, pred[]{:T(512)S(6)} %compare.5, bf16[2432,1792]{1,0:T(8,128)(2,1)} %get-tuple-element.226, s32[]{:T(128)S(6)} %select_n.41, bf16[2432,1024]{1,0:T(8,128)(2,1)} %get-tuple-element.225, pred[384]{0:T(512)(128)(4,1)S(1)} %iota_compare_fusion.2), kind=kOutput, calls=%fused_computation.2.clone.1 | convolution fusion | flops 1415184384 | bytes 16844672 | tf_op jit(solution)/shard_map/while/body/eval_jaxpr/dot_general | solution.py:29
  244.1 9.0 %select_add_fusion.2 = f32[1024,1792]{1,0:T(8,128)} fusion(f32[1024,1792]{1,0:T(8,128)} %get-tuple-element.213, pred[]{:T(512)S(6)} %compare.5, bf16[2432,1792]{1,0:T(8,128)(2,1)} %get-tuple-element.226, s32[]{:T(128)S(6)} %select_n.41, bf16[2432,1024]{1,0:T(8,128)(2,1)} %get-tuple-element.225, pred[384]{0:T(512)(128)(4,1)S(1)} %iota_compare_fusion.2), kind=kOutput, calls=%fused_computation.2.clone.1 | convolution fusion | flops 1415184384 | bytes 16844672 | tf_op jit(solution)/shard_map/while/body/eval_jaxpr/dot_general | solution.py:29
  256.9 9.0 %select_add_fusion.2 = f32[1024,1792]{1,0:T(8,128)} fusion(f32[1024,1792]{1,0:T(8,128)} %get-tuple-element.213, pred[]{:T(512)S(6)} %compare.5, bf16[2432,1792]{1,0:T(8,128)(2,1)} %get-tuple-element.226, s32[]{:T(128)S(6)} %select_n.41, bf16[2432,1024]{1,0:T(8,128)(2,1)} %get-tuple-element.225, pred[384]{0:T(512)(128)(4,1)S(1)} %iota_compare_fusion.2), kind=kOutput, calls=%fused_computation.2.clone.1 | convolution fusion | flops 1415184384 | bytes 16844672 | tf_op jit(solution)/shard_map/while/body/eval_jaxpr/dot_general | solution.py:29
  266.0 0.6 dynamic_slice.45
  269.8 9.0 %select_add_fusion.2 = f32[1024,1792]{1,0:T(8,128)} fusion(f32[1024,1792]{1,0:T(8,128)} %get-tuple-element.213, pred[]{:T(512)S(6)} %compare.5, bf16[2432,1792]{1,0:T(8,128)(2,1)} %get-tuple-element.226, s32[]{:T(128)S(6)} %select_n.41, bf16[2432,1024]{1,0:T(8,128)(2,1)} %get-tuple-element.225, pred[384]{0:T(512)(128)(4,1)S(1)} %iota_compare_fusion.2), kind=kOutput, calls=%fused_computation.2.clone.1 | convolution fusion | flops 1415184384 | bytes 16844672 | tf_op jit(solution)/shard_map/while/body/eval_jaxpr/dot_general | solution.py:29
  278.8 10.4 %broadcast_add_fusion = (f32[1024,1792]{1,0:T(8,128)}, f32[1024,1792]{1,0:T(8,128)}) fusion(f32[1024,1792]{1,0:T(8,128)} %get-tuple-element.126, bf16[1,1,1024,1792]{3,2,1,0:T(8,128)(2,1)} %param.11), kind=kLoop, calls=%fused_computation.12 | loop fusion | flops 5505024 | bytes 25690112 | tf_op jit(solution)/shard_map/add | solution.py:59
  289.3 0.7 reduce-scatter.3.cloned.1.call-update
  290.0 90.3 %reduce-scatter.5.cloned.1.call-done = f32[256,1792]{1,0:T(8,128)} async-done(((f32[1024,1792]{1,0:T(8,128)}), f32[256,1792]{1,0:T(8,128)}) %reduce-scatter.5.cloned.1.call-update) | async-done | bytes 1835024 | tf_op jit(solution)/shard_map/reduce_scatter | solution.py:66
  380.3 74.7 %reduce-scatter.3.cloned.1.call-done = f32[256,1792]{1,0:T(8,128)} async-done(((f32[1024,1792]{1,0:T(8,128)}), f32[256,1792]{1,0:T(8,128)}) %reduce-scatter.3.cloned.1.call-update) | async-done | bytes 1835024 | tf_op jit(solution)/shard_map/reduce_scatter | solution.py:63
  455.0 3.8 multiply_bitcast_fusion
  (33 shorter events, 11.6 us)
Async XLA Ops:
  8.6 12.2 %copy-start = (bf16[1,64,14336]{2,1,0:T(8,128)(2,1)S(1)}, bf16[1,64,14336]{2,1,0:T(8,128)(2,1)}, u32[]{:S(2)}) copy-start(bf16[1,64,14336]{2,1,0:T(8,128)(2,1)} %param.10) | copy-start | bytes 5505028
  11.3 61.7 %all-to-all-start = ((bf16[64,32,1024]{2,0,1:T(8,128)(2,1)}), bf16[64,32,1024]{2,0,1:T(8,128)(2,1)}, u32[]{:S(2)}, u32[]{:S(2)}) async-start(bf16[64,32,1024]{2,0,1:T(8,128)(2,1)} %bitcast.29), calls=%async_computation | async-start | bytes 8388608 | tf_op jit(solution)/shard_map/all_to_all | solution.py:49
  50.3 30.1 %copy-start.2 = (s32[1,8]{1,0:T(1,128)S(1)}, s32[1,8]{1,0:T(1,128)}, u32[]{:S(2)}) copy-start(s32[1,8]{1,0:T(1,128)} %param.9) | copy-start | bytes 100
  50.3 30.3 %copy-start.1 = (s32[1,2048]{1,0:T(1,128)S(1)}, s32[1,2048]{1,0:T(1,128)}, u32[]{:S(2)}) copy-start(s32[1,2048]{1,0:T(1,128)} %param.8) | copy-start | bytes 24580
  73.0 98.3 %all-to-all-start.1 = ((bf16[64,32,1792]{2,0,1:T(8,128)(2,1)}), bf16[64,32,1792]{2,0,1:T(8,128)(2,1)}, u32[]{:S(2)}, u32[]{:S(2)}) async-start(bf16[64,32,1792]{2,0,1:T(8,128)(2,1)} %copy.12), calls=%async_computation.1 | async-start | bytes 14680064 | tf_op jit(solution)/shard_map/all_to_all | solution.py:57
  80.2 300.1 %reduce-scatter.5.cloned.1.call-start = ((), (), s32[]{:S(2)}) async-start(), calls=%async_computation.5 | async-start | bytes 9175040 | tf_op jit(solution)/shard_map/reduce_scatter | solution.py:66
  289.2 165.7 %reduce-scatter.3.cloned.1.call-start = ((), (), s32[]{:S(2)}) async-start(), calls=%async_computation.4 | async-start | bytes 9175040 | tf_op jit(solution)/shard_map/reduce_scatter | solution.py:63
Sparse Core Ops, SparseCore 0:
  289.4 90.9 reduce-scatter.4
  382.7 72.2 reduce-scatter.2
where the time goes:
time: 467 us; the launch traced here: 466 us
  waiting for transfers between devices  260 us (56%)
  matrix products  70.1 us (15%)
  local copies, waits for them, and re-layouts  69.1 us (15%)
  other arithmetic  19.5 us (4%)
  starting transfers between devices  16.9 us (4%)
  loops' own time  15.6 us (3%)
  between operations  14.1 us (3%)
    reduce_scatter x1, waiting for transfers between devices, body(): lax.psum_scatter(fisher_mass, 'ckpt', scatter_dimension=0, tiled=True)  90.3 us
    reduce_scatter x1, waiting for transfers between devices, body(): lax.psum_scatter(fisher_mass * own_weight.astype(jnp.float32), 'ckpt', sc...  74.7 us
    all_to_all x1, waiting for transfers between devices, body(): lax.all_to_all(grad_parts, 'fsdp', split_axis=1, concat_axis=0, tiled=True)  71.9 us
    dot_general x8, matrix products, add_example(): lax.dot_general(act_block, grad_block, (((0,), (0,)), ((), ())), preferre...  70.1 us
    all_to_all x2, local copies, waits for them, and re-layouts, body(): lax.all_to_all(grad_parts, 'fsdp', split_axis=1, concat_axis=0, tiled=True)  23.4 us
    all_to_all x1, waiting for transfers between devices, body(): lax.all_to_all(act_parts, 'fsdp', split_axis=1, concat_axis=0, tiled=True)  22.7 us
    another operation x1, loops' own time, example_fisher(): return lax.fori_loop(0, example_lengths.shape[0], add_example, start_value)  15.6 us
    gather x1, local copies, waits for them, and re-layouts, body(): act_rows = table_rows[token_ids[0]]  13.7 us
  transfers between devices with their start and end apart: 4, of which 4 were waited for; matrix products, arithmetic and copies ran while one was open for 8% of the time, Pallas kernels for 0%

commit v1 on v0

v1 whole, which is shorter than its diff:
```python
import jax
import jax.numpy as jnp
from jax import lax
from jax.experimental import pallas as pl
from jax.experimental.pallas import tpu as pltpu
from jax.sharding import PartitionSpec as P

PRIOR = 0.1
ROWS = 512
SPANS = (
    (0, 384), (0, 768), (0, 1152), (128, 1536), (512, 1920), (896, 2048), (1280, 2048), (1664, 2048),
)
CHUNKS = (256,) * 7
LOW, HIGH = -3.32195, 20.04
LN2 = 0.6931471805599453
SCALE = 65535.0 / (HIGH - LOW)
MESH = pl.DeviceIdType.MESH


def kernel(
    act, ids, lengths, grads, weights, merged, mean_mass,
    piece, rows_t, act_t, windows, fisher, own_w, got_w, own_mass, sent, got, blocks,
    a_send, a_recv, g_send, g_recv, z_send, z_recv, x_send, x_recv, w_send, w_recv, m_send, m_recv, own_sem,
):
    me = lax.axis_index("fsdp")
    y = lax.axis_index("ckpt")
    x, zc = me // 8, me % 8
    z, c = zc // 2, zc % 2
    up, down = (z + 1) % 4, (z + 3) % 4
    right, left = (x + 1) % 4, (x + 3) % 4
    offsets = [sum(CHUNKS[:j]) for j in range(len(CHUNKS))]
    n = len(CHUNKS)
    width = sum(CHUNKS)

    def plane(index):
        return {"fsdp": index, "ckpt": y}

    def column(index):
        return {"fsdp": me, "ckpt": index}

    barrier = pltpu.get_barrier_semaphore()

    @pl.loop(1, 32)
    def _(k):
        pl.semaphore_signal(barrier, inc=1, device_id=plane((me + k) % 32), device_id_type=MESH)

    for d in range(1, 4):
        pl.semaphore_signal(barrier, inc=1, device_id=column((y + d) % 4), device_id_type=MESH)
    pl.semaphore_wait(barrier, 34)

    def remote(src, dst, send, recv, target):
        return pltpu.make_async_remote_copy(
            src_ref=src, dst_ref=dst, send_sem=send, recv_sem=recv, device_id=target, device_id_type=MESH
        )

    def sized(ref, sem):
        pltpu.make_async_copy(ref, ref, sem).wait()

    def z_start(j):
        wide = CHUNKS[j]
        dst = blocks[j].at[pl.ds(pl.multiple_of(me * 64, 64), 64)]

        def src(block):
            return grads.at[0, :, pl.ds(pl.multiple_of(block * width + offsets[j], 128), wide)]

        @pl.loop(1, 8)
        def _(k):
            other = (zc + k) % 8
            remote(src(other), dst, z_send.at[j], z_recv.at[j], plane(x * 8 + other)).start()

        pltpu.make_async_copy(src(zc), dst, z_recv.at[j]).start()

    def band(j, which, first=0, count=512):
        return blocks[j].at[pl.ds(pl.multiple_of(which * 512 + first, 64), count)]

    x_targets = {0: right, 1: left, 2: right, 3: left}

    def x_copy(j, i):
        part = (band(j, x), band(j, x), band(j, left, 0, 256), band(j, right, 256, 256))[i]
        return remote(part, part, x_send.at[j, i], x_recv.at[j, i], plane(x_targets[i] * 8 + zc))

    def x_arrived(j, i):
        part = (band(j, left), band(j, right), band(j, (x + 2) % 4, 0, 256), band(j, (x + 2) % 4, 256, 256))[i]
        sized(part, x_recv.at[j, i])

    def x_start(j):
        sized(band(j, x), z_recv.at[j])
        x_copy(j, 0).start()
        x_copy(j, 1).start()

    def x_pass(j):
        x_arrived(j, 0)
        x_copy(j, 2).start()
        x_arrived(j, 1)
        x_copy(j, 3).start()

    def x_finish(j):
        x_arrived(j, 2)
        x_arrived(j, 3)

    def a_source(target):
        return act.at[0, :, pl.ds(pl.multiple_of(target * 128, 128), 128)]

    z_start(0)
    a_rows = piece.at[pl.ds(pl.multiple_of(me * 64, 64), 64)]

    @pl.loop(1, 32)
    def _(k):
        target = (me + k) % 32
        remote(a_source(target), a_rows, a_send, a_recv, plane(target)).start()

    pltpu.make_async_copy(a_source(me), a_rows, a_recv).start()

    def w_rows(owner):
        return weights.at[0, 0, pl.ds(pl.multiple_of(owner * 256, 256), 256)]

    w_copies = [
        remote(w_rows((y + d) % 4), got_w.at[d - 1], w_send.at[d - 1], w_recv.at[d - 1], column((y + d) % 4))
        for d in range(1, 4)
    ]
    z_start(1)
    for copy in w_copies:
        copy.start()
    own_copy = pltpu.make_async_copy(w_rows(y), own_w, own_sem)
    own_copy.start()
    for j in range(2, n):
        z_start(j)

    first_of = [jnp.int32(0)]
    for e in range(8):
        first_of.append(first_of[e] + lengths[0, e])

    x_start(0)
    sized(piece, a_recv)

    @pl.loop(0, 8)
    def _(b):
        at = pl.ds(pl.multiple_of(b * 256, 256), 256)
        rows_t[:, at] = piece[at, :].astype(jnp.float32).T.astype(jnp.bfloat16)

    x_start(1)

    @pl.loop(0, 8)
    def _(b):
        at = pl.ds(pl.multiple_of(b * 256, 256), 256)
        hot = lax.broadcasted_iota(jnp.int32, (2048, 256), 0) == ids[:, at]
        hot = jnp.where(hot, jnp.float32(1), jnp.float32(0)).astype(jnp.bfloat16)
        placed = jnp.dot(rows_t[...], hot, preferred_element_type=jnp.float32)
        act_t[zc, :, at] = placed.astype(jnp.bfloat16)

    other_core = plane(x * 8 + z * 2 + 1 - c)

    def g_copy(i):
        own, below, above, far = (
            act_t.at[zc], act_t.at[down * 2 + c], act_t.at[up * 2 + c], act_t.at[((z + 2) % 4) * 2 + c],
        )
        part, target = (
            (own, plane(x * 8 + up * 2 + c)),
            (own, plane(x * 8 + down * 2 + c)),
            (below.at[pl.ds(0, 64)], plane(x * 8 + up * 2 + c)),
            (above.at[pl.ds(64, 64)], plane(x * 8 + down * 2 + c)),
            (own, other_core),
            (below, other_core),
            (above, other_core),
            (far, other_core),
        )[i]
        return remote(part, part, g_send.at[i], g_recv.at[i], target)

    def g_arrived(i):
        o = 1 - c
        far = act_t.at[((z + 2) % 4) * 2 + c]
        part = (
            act_t.at[down * 2 + c], act_t.at[up * 2 + c], far.at[pl.ds(0, 64)], far.at[pl.ds(64, 64)],
            act_t.at[z * 2 + o], act_t.at[down * 2 + o], act_t.at[up * 2 + o], act_t.at[((z + 2) % 4) * 2 + o],
        )[i]
        sized(part, g_recv.at[i])

    for i in (0, 1, 4):
        g_copy(i).start()
    x_pass(0)
    x_start(2)
    g_arrived(0)
    g_copy(2).start()
    g_copy(5).start()
    g_arrived(1)
    g_copy(3).start()
    g_copy(6).start()
    x_pass(1)
    g_arrived(2)
    g_arrived(3)
    g_copy(7).start()
    x_start(3)
    for i in (4, 5, 6, 7):
        g_arrived(i)

    for e, (low, high) in enumerate(SPANS):
        position = low + lax.broadcasted_iota(jnp.int32, (1, high - low), 1)
        keep = (position >= first_of[e]) & (position < first_of[e] + lengths[0, e])
        keep = jnp.where(keep, jnp.float32(1), jnp.float32(0)).astype(jnp.bfloat16)

        @pl.loop(0, 8)
        def _(q):
            windows[e][pl.ds(pl.multiple_of(q * 128, 128), 128), :] = act_t[q, :, low:high] * keep

    def compute(j):
        wide = CHUNKS[j]

        @pl.loop(0, 1024 // ROWS)
        def _(q):
            at = pl.ds(pl.multiple_of(q * ROWS, ROWS), ROWS)
            for e, (low, high) in enumerate(SPANS):
                part = jnp.dot(windows[e][at, :], blocks[j][low:high, :], preferred_element_type=jnp.float32)
                part = part * part
                fisher[at, :wide] = part + (PRIOR if e == 0 else fisher[at, :wide])

        @pl.loop(0, 4)
        def _(q):
            at = pl.ds(pl.multiple_of(q * 256, 256), 256)
            code = jnp.log(fisher[at, :wide]) * (SCALE / LN2) - (LOW * SCALE + 32767.5)
            code = jnp.clip(jnp.floor(code), -32768.0, 32767.0).astype(jnp.int32)
            sent[j][at, :] = code.astype(jnp.int16)

        own_mass[:, offsets[j] : offsets[j] + wide] = fisher[pl.ds(pl.multiple_of(y * 256, 256), 256), :wide]

    def m_copy(j, d):
        owner = (y + d) % 4
        return remote(
            sent[j].at[pl.ds(pl.multiple_of(owner * 256, 256), 256)],
            got[j].at[d - 1], m_send.at[j, d - 1], m_recv.at[j, d - 1], column(owner),
        )

    def combine(j):
        columns = slice(offsets[j], offsets[j] + CHUNKS[j])
        for d in range(1, 4):
            sized(got[j].at[d - 1], m_recv.at[j, d - 1])

        @pl.loop(0, 8)
        def _(q):
            at = pl.ds(pl.multiple_of(q * 32, 32), 32)
            total = own_mass[at, columns]
            weighted = total * own_w[at, columns].astype(jnp.float32)
            for d in range(3):
                code = got[j][d, at, :].astype(jnp.int32).astype(jnp.float32)
                mass = jnp.exp((code + (32768.0 + LOW * SCALE)) * (LN2 / SCALE))
                total += mass
                weighted += mass * got_w[d, at, columns].astype(jnp.float32)
            merged[0, at, columns] = (weighted / total).astype(jnp.bfloat16)
            mean_mass[0, at, columns] = total * 0.25

    for j in range(n):
        if j + 1 < n and j > 0:
            x_pass(j + 1)
        if j + 3 < n and j > 0:
            x_start(j + 3)
        x_finish(j)
        compute(j)
        for d in range(1, 4):
            m_copy(j, d).start()
        if j == 0:
            own_copy.wait()
            for i in range(3):
                sized(got_w.at[i], w_recv.at[i])
        if j >= 2:
            combine(j - 2)
    combine(n - 2)
    combine(n - 1)

    pltpu.make_async_copy(piece.at[pl.ds(0, 31 * 64)], piece.at[pl.ds(0, 31 * 64)], a_send).wait()
    for copy in w_copies:
        copy.wait_send()
    for i in range(8):
        g_copy(i).wait_send()
    for j in range(n):
        sized(blocks[j].at[pl.ds(0, 7 * 64)], z_send.at[j])
        for i in range(4):
            x_copy(j, i).wait_send()
        for d in range(1, 4):
            m_copy(j, d).wait_send()


def body(act_table, token_ids, lengths, grads, weights):
    n = len(CHUNKS)
    wide = sum(CHUNKS)
    dma = pltpu.SemaphoreType.DMA
    whole = pl.BlockSpec(memory_space=pltpu.VMEM)
    anywhere = pl.BlockSpec(memory_space=pl.ANY)
    return pl.pallas_call(
        kernel,
        out_shape=(
            jax.ShapeDtypeStruct((1, 256, wide), jnp.bfloat16),
            jax.ShapeDtypeStruct((1, 256, wide), jnp.float32),
        ),
        in_specs=[anywhere, whole, pl.BlockSpec(memory_space=pltpu.SMEM), anywhere, anywhere],
        out_specs=(whole, whole),
        scratch_shapes=[
            pltpu.VMEM((2048, 128), jnp.bfloat16),
            pltpu.VMEM((128, 2048), jnp.bfloat16),
            pltpu.VMEM((8, 128, 2048), jnp.bfloat16),
            tuple(pltpu.VMEM((1024, high - low), jnp.bfloat16) for low, high in SPANS),
            pltpu.VMEM((1024, max(CHUNKS)), jnp.float32),
            pltpu.VMEM((256, wide), jnp.bfloat16),
            pltpu.VMEM((3, 256, wide), jnp.bfloat16),
            pltpu.VMEM((256, wide), jnp.float32),
            tuple(pltpu.VMEM((1024, w), jnp.int16) for w in CHUNKS),
            tuple(pltpu.VMEM((3, 256, w), jnp.int16) for w in CHUNKS),
            tuple(pltpu.VMEM((2048, w), jnp.bfloat16) for w in CHUNKS),
            dma, dma, dma((8,)), dma((8,)), dma((n,)), dma((n,)), dma((n, 4)), dma((n, 4)),
            dma((3,)), dma((3,)), dma((n, 3)), dma((n, 3)), dma,
        ],
        compiler_params=pltpu.CompilerParams(
            collective_id=0, has_side_effects=True, vmem_limit_bytes=58 << 20
        ),
    )(act_table, token_ids, lengths, grads, weights)


def solution(mesh):
    placed = (
        P("ckpt", "fsdp", None),
        P("ckpt", None),
        P("ckpt", None),
        P("ckpt", "fsdp", None),
        P("ckpt", "fsdp", None, None),
    )
    return jax.shard_map(
        body,
        mesh=mesh,
        in_specs=placed,
        out_specs=(P("fsdp", "ckpt", None), P("fsdp", "ckpt", None)),
        check_vma=False,
    )
```

time: 467 us -> 121 us (0.26)
  waiting for transfers between devices: 260 us -> 0 us
  Pallas kernels: 0 us -> 116 us
  matrix products: 70.1 us -> 0 us
  local copies, waits for them, and re-layouts: 69.1 us -> 3.53 us
  other arithmetic: 19.5 us -> 0 us
  starting transfers between devices: 16.9 us -> 0 us
  loops' own time: 15.6 us -> 0 us
  between operations: 14.1 us -> 0.65 us
    reduce_scatter x2 -> x0, waiting for transfers between devices: 165 us -> none  [the longest x1 90.3 us: body(): lax.psum_scatter(fisher_mass, 'ckpt', scatter_dimension=0, tiled=True)]
    pallas_call x0 -> x1, Pallas kernels: none -> 116 us  [body(): pl.pallas_call(kernel, out_shape=(jax.ShapeDtypeStruct((1, 256, wide), jn...]
    all_to_all x2 -> x0, waiting for transfers between devices: 94.6 us -> none  [the longest x1 71.9 us: body(): lax.all_to_all(grad_parts, 'fsdp', split_axis=1, concat_axis=0, tiled=True)]
    dot_general x8 -> x0, matrix products: 70.1 us -> none  [add_example(): lax.dot_general(act_block, grad_block, (((0,), (0,)), ((), ())), preferre...]
    all_to_all x2 -> x0, local copies, waits for them, and re-layouts: 23.4 us -> none  [body(): lax.all_to_all(grad_parts, 'fsdp', split_axis=1, concat_axis=0, tiled=True)]
    all_to_all x2 -> x0, starting transfers between devices: 16.6 us -> none  [the longest x1 9.49 us: body(): lax.all_to_all(act_parts, 'fsdp', split_axis=1, concat_axis=0, tiled=True)]
    another operation x1 -> x0, loops' own time: 15.6 us -> none  [example_fisher(): return lax.fori_loop(0, example_lengths.shape[0], add_example, start_value)]
    gather x1 -> x0, local copies, waits for them, and re-layouts: 13.7 us -> none  [body(): act_rows = table_rows[token_ids[0]]]
  transfers between devices with their start and end apart: 4 -> 0, of which waited for: 4 -> 0; matrix products, arithmetic and copies ran while one was open for 8% -> 0% of each run, Pallas kernels for 0% -> 0%
where the time goes in v1:
time: 121 us; the launch traced here: 120 us
  Pallas kernels  116 us (96%)
  local copies, waits for them, and re-layouts  3.53 us (3%)
    pallas_call x1, Pallas kernels, body(): pl.pallas_call(kernel, out_shape=(jax.ShapeDtypeStruct((1, 256, wide), jn...  116 us
    unnamed x4, local copies, waits for them, and re-layouts  3.53 us

profile of v1, /device:TPU:1, one launch (start us, length us, event | category | flops | bytes accessed | tf_op | source)
XLA Modules:
  0.0 120.5 jit_solution(9818265846608225025)
XLA Ops:
  0.6 116.3 %shard_map.68 = (bf16[1,256,1792]{2,1,0:T(8,128)(2,1)}, f32[1,256,1792]{2,1,0:T(8,128)}) custom-call(bf16[1,64,4096]{2,1,0:T(8,128)(2,1)} %act.1, s32[1,2048]{1,0:T(1,128)} %ids.1, s32[1,8]{1,0:T(1,128)} %lengths.1, bf16[1,64,14336]{2,1,0:T(8,128)(2,1)} %grads.1, bf16[1,1,1024,1792]{3,2,1,0:T(8,128)(2,1)} %weights.1), custom_call_target="tpu_custom_call" | custom-call | tf_op jit(solution)/shard_map/pallas_call | solution.py:287
  116.9 0.0 copy-start
  117.0 2.3 %copy.9 = bf16[1,256,1792]{2,1,0:T(8,128)(2,1)} copy(bf16[1,256,1792]{2,1,0:T(8,128)(2,1)} %get-tuple-element.4) | data formatting | bytes 1835008
  119.3 0.0 copy-done
  119.3 1.2 %copy.10 = f32[1,256,1792]{2,1,0:T(8,128)} copy(f32[1,256,1792]{2,1,0:T(8,128)S(1)} %copy-done) | data formatting | bytes 3670016
Async XLA Ops:
  116.9 2.3 %copy-start = (f32[1,256,1792]{2,1,0:T(8,128)S(1)}, f32[1,256,1792]{2,1,0:T(8,128)}, u32[]{:S(2)}) copy-start(f32[1,256,1792]{2,1,0:T(8,128)} %get-tuple-element.5) | copy-start | bytes 5505028

commit v2 on v1

v2 whole, which is shorter than its diff:
```python
import jax
import jax.numpy as jnp
from jax import lax
from jax.experimental import pallas as pl
from jax.experimental.pallas import tpu as pltpu
from jax.sharding import PartitionSpec as P

PRIOR = 0.1
CHUNKS = (256,) * 6 + (128,) * 2
LOW, HIGH = -3.32195, 20.04
LN2 = 0.6931471805599453
SCALE = 65535.0 / (HIGH - LOW)
MESH = pl.DeviceIdType.MESH
ORDER = (
    "A", "z0", "W", "z1", "H", "z2", "s0", "s1", "T", "P", "G", "z3", "s2", "p0", "X", "B", "U", "z4",
    "s3", "p1", "F", "z5", "Y", "Z", "s4", "p2", "z6", "z7", "f0", "c0", "p3", "s5", "f1", "c1", "p4",
    "s6", "f2", "c2", "V", "o0", "p5", "s7", "f3", "c3", "o1", "p6", "f4", "c4", "o2", "p7", "f5", "c5",
    "o3", "f6", "c6", "o4", "f7", "c7", "o5", "o6", "o7",
)


def kernel(
    act, ids, lengths, grads, weights, merged, mean_mass,
    piece, rows_t, act_t, windows, framed, fisher, own_w, got_w, own_mass, sent, got, blocks,
    a_send, a_recv, g_send, g_recv, z_send, z_recv, x_send, x_recv, w_send, w_recv, m_send, m_recv, own_sem,
):
    me = lax.axis_index("fsdp")
    y = lax.axis_index("ckpt")
    x, zc = me // 8, me % 8
    z, c = zc // 2, zc % 2
    up, down = (z + 1) % 4, (z + 3) % 4
    right, left = (x + 1) % 4, (x + 3) % 4
    offsets = [sum(CHUNKS[:j]) for j in range(len(CHUNKS))]
    n = len(CHUNKS)
    width = sum(CHUNKS)

    def plane(index):
        return {"fsdp": index, "ckpt": y}

    def column(index):
        return {"fsdp": me, "ckpt": index}

    barrier = pltpu.get_barrier_semaphore()

    @pl.loop(1, 32)
    def _(k):
        pl.semaphore_signal(barrier, inc=1, device_id=plane((me + k) % 32), device_id_type=MESH)

    for d in range(1, 4):
        pl.semaphore_signal(barrier, inc=1, device_id=column((y + d) % 4), device_id_type=MESH)
    pl.semaphore_wait(barrier, 34)

    def remote(src, dst, send, recv, target):
        return pltpu.make_async_remote_copy(
            src_ref=src, dst_ref=dst, send_sem=send, recv_sem=recv, device_id=target, device_id_type=MESH
        )

    def sized(ref, sem):
        pltpu.make_async_copy(ref, ref, sem).wait()

    def z_start(j):
        wide = CHUNKS[j]
        dst = blocks[j].at[me // 2, pl.ds(pl.multiple_of((me % 2) * 64, 64), 64)]

        def src(block):
            return grads.at[0, :, pl.ds(pl.multiple_of(block * width + offsets[j], 128), wide)]

        @pl.loop(1, 8)
        def _(k):
            other = (zc + k) % 8
            remote(src(other), dst, z_send.at[j], z_recv.at[j], plane(x * 8 + other)).start()

        pltpu.make_async_copy(src(zc), dst, z_recv.at[j]).start()

    def band(j, which, first=0, count=4):
        return blocks[j].at[pl.ds(which * 4 + first, count)]

    x_targets = {0: right, 1: left, 2: right, 3: left}

    def x_copy(j, i):
        part = (band(j, x), band(j, x), band(j, left, 0, 2), band(j, right, 2, 2))[i]
        return remote(part, part, x_send.at[j, i], x_recv.at[j, i], plane(x_targets[i] * 8 + zc))

    def x_arrived(j, i):
        part = (band(j, left), band(j, right), band(j, (x + 2) % 4, 0, 2), band(j, (x + 2) % 4, 2, 2))[i]
        sized(part, x_recv.at[j, i])

    def x_start(j):
        sized(band(j, x), z_recv.at[j])
        x_copy(j, 0).start()
        x_copy(j, 1).start()

    def x_pass(j):
        x_arrived(j, 0)
        x_copy(j, 2).start()
        x_arrived(j, 1)
        x_copy(j, 3).start()

    def x_finish(j):
        x_arrived(j, 2)
        x_arrived(j, 3)

    def a_source(target):
        return act.at[0, :, pl.ds(pl.multiple_of(target * 128, 128), 128)]

    a_rows = piece.at[pl.ds(pl.multiple_of(me * 64, 64), 64)]

    def a_start():
        @pl.loop(1, 32)
        def _(k):
            target = (me + k) % 32
            remote(a_source(target), a_rows, a_send, a_recv, plane(target)).start()

        pltpu.make_async_copy(a_source(me), a_rows, a_recv).start()

    def w_rows(owner):
        return weights.at[0, 0, pl.ds(pl.multiple_of(owner * 256, 256), 256)]

    w_copies = [
        remote(w_rows((y + d) % 4), got_w.at[d - 1], w_send.at[d - 1], w_recv.at[d - 1], column((y + d) % 4))
        for d in range(1, 4)
    ]
    own_copy = pltpu.make_async_copy(w_rows(y), own_w, own_sem)

    def w_start():
        for copy in w_copies:
            copy.start()
        own_copy.start()

    def w_arrived():
        own_copy.wait()
        for i in range(3):
            sized(got_w.at[i], w_recv.at[i])

    first_of = [jnp.int32(0)]
    for e in range(8):
        first_of.append(first_of[e] + lengths[0, e])

    lead, keeps = [], []
    for e in range(8):
        lead.append(jnp.minimum(first_of[e] // 128, 12))
        position = lead[e] * 128 + lax.broadcasted_iota(jnp.int32, (1, 512), 1)
        keep = (position >= first_of[e]) & (position < first_of[e] + lengths[0, e])
        keeps.append(jnp.where(keep, jnp.float32(1), jnp.float32(0)).astype(jnp.bfloat16))

    def a_turn():
        sized(piece, a_recv)

        @pl.loop(0, 8)
        def _(b):
            at = pl.ds(pl.multiple_of(b * 256, 256), 256)
            rows_t[:, at] = piece[at, :].astype(jnp.float32).T.astype(jnp.bfloat16)

    def hot_build():
        @pl.loop(0, 8)
        def _(b):
            own = ids[:, pl.ds(pl.multiple_of(b * 256, 256), 256)]
            for h in range(2):
                hot = lax.broadcasted_iota(jnp.int32, (1024, 256), 0) + h * 1024 == own
                hot = jnp.where(hot, jnp.float32(1), jnp.float32(0)).astype(jnp.bfloat16)
                windows[b, :, h * 256 : (h + 1) * 256] = hot

    def a_permute():
        @pl.loop(0, 8)
        def _(b):
            placed = sum(
                jnp.dot(
                    rows_t[:, h * 1024 : (h + 1) * 1024],
                    windows[b, :, h * 256 : (h + 1) * 256],
                    preferred_element_type=jnp.float32,
                )
                for h in range(2)
            )
            for i in range(2):
                act_t[0][b * 2 + i] = placed[:, i * 128 : (i + 1) * 128].astype(jnp.bfloat16)

    above_core, below_core = plane(x * 8 + up * 2 + c), plane(x * 8 + down * 2 + c)
    other_core = plane(x * 8 + z * 2 + 1 - c)
    first_half, second_half = pl.ds(0, 8), pl.ds(8, 8)

    def g_copy(i):
        src, dst, target = (
            (act_t[0], act_t[1], above_core),
            (act_t[0], act_t[2], below_core),
            (act_t[1].at[first_half], act_t[3].at[first_half], above_core),
            (act_t[2].at[second_half], act_t[3].at[second_half], below_core),
            (act_t[0], act_t[4], other_core),
            (act_t[1], act_t[5], other_core),
            (act_t[2], act_t[6], other_core),
            (act_t[3], act_t[7], other_core),
        )[i]
        return remote(src, dst, g_send.at[i], g_recv.at[i], target)

    def g_arrived(i):
        part = (
            act_t[1], act_t[2], act_t[3].at[first_half], act_t[3].at[second_half],
            act_t[4], act_t[5], act_t[6], act_t[7],
        )[i]
        sized(part, g_recv.at[i])

    def mask(k):
        owner = (z + (0, 3, 1, 2)[k % 4]) % 4 * 2 + (c if k < 4 else 1 - c)
        for e in range(8):
            for i in range(4):
                at = slice(i * 128, (i + 1) * 128)
                rows = pl.ds(pl.multiple_of(owner * 128, 128), 128)
                windows[e, rows, at] = act_t[k][lead[e] + i] * keeps[e][:, at]

    def g_start():
        for i in (0, 1, 4):
            g_copy(i).start()

    def g_below():
        g_arrived(0)
        g_copy(2).start()
        g_copy(5).start()

    def g_above():
        g_arrived(1)
        g_copy(3).start()
        g_copy(6).start()

    def g_far():
        g_arrived(2)
        g_arrived(3)
        g_copy(7).start()

    def mask_own():
        mask(0)
        g_arrived(4)
        mask(4)

    def mask_near():
        mask(1)
        mask(2)
        g_arrived(5)
        mask(5)
        g_arrived(6)
        mask(6)

    def mask_far():
        mask(3)
        g_arrived(7)
        mask(7)

    def m_copy(j, d):
        owner = (y + d) % 4
        return remote(
            sent[j].at[pl.ds(pl.multiple_of(owner * 256, 256), 256)],
            got[j].at[d - 1], m_send.at[j, d - 1], m_recv.at[j, d - 1], column(owner),
        )

    def rows_of(j, owner):
        wide = CHUNKS[j]
        at = pl.ds(pl.multiple_of(owner * 256, 256), 256)
        for e in range(8):
            part = jnp.dot(windows[e, at, :], framed[e, :, :wide], preferred_element_type=jnp.float32)
            part = part * part
            fisher[:, :wide] = part + (PRIOR if e == 0 else fisher[:, :wide])

        @pl.when(owner != y)
        def _():
            code = jnp.log(fisher[:, :wide]) * (SCALE / LN2) - (LOW * SCALE + 32767.5)
            code = jnp.clip(jnp.floor(code), -32768.0, 32767.0).astype(jnp.int32)
            sent[j][at, :] = code.astype(jnp.int16)
            m_copy(j, (owner + 4 - y) % 4).start()

        @pl.when(owner == y)
        def _():
            own_mass[:, offsets[j] : offsets[j] + wide] = fisher[:, :wide]

    def frame(j):
        for e in range(8):
            for i in range(4):
                framed[e, i * 128 : (i + 1) * 128, : CHUNKS[j]] = blocks[j][lead[e] + i]

    def compute(j):
        frame(j)

        @pl.loop(0, 4)
        def _(t):
            rows_of(j, (y + ((t + 1) % 3 + 1) * (1 - t // 3)) % 4)

    def combine(j):
        columns = slice(offsets[j], offsets[j] + CHUNKS[j])
        for d in range(1, 4):
            sized(got[j].at[d - 1], m_recv.at[j, d - 1])

        @pl.loop(0, 8)
        def _(q):
            at = pl.ds(pl.multiple_of(q * 32, 32), 32)
            total = own_mass[at, columns]
            weighted = total * own_w[at, columns].astype(jnp.float32)
            for d in range(3):
                code = got[j][d, at, :].astype(jnp.int32).astype(jnp.float32)
                mass = jnp.exp((code + (32768.0 + LOW * SCALE)) * (LN2 / SCALE))
                total += mass
                weighted += mass * got_w[d, at, columns].astype(jnp.float32)
            merged[0, at, columns] = (weighted / total).astype(jnp.bfloat16)
            mean_mass[0, at, columns] = total * 0.25

    steps = {
        "z": z_start, "s": x_start, "p": x_pass, "f": x_finish, "c": compute, "o": combine,
        "A": a_start, "W": w_start, "V": w_arrived, "T": a_turn, "H": hot_build, "P": a_permute, "G": g_start, "B": g_below,
        "U": g_above, "F": g_far, "X": mask_own, "Y": mask_near, "Z": mask_far,
    }
    for step in ORDER:
        steps[step[0]](*(int(j) for j in step[1:]))

    pltpu.make_async_copy(piece.at[pl.ds(0, 31 * 64)], piece.at[pl.ds(0, 31 * 64)], a_send).wait()
    for copy in w_copies:
        copy.wait_send()
    for i in range(8):
        g_copy(i).wait_send()
    for j in range(n):
        sized(blocks[j].at[pl.ds(0, 7), pl.ds(0, 64)], z_send.at[j])
        for i in range(4):
            x_copy(j, i).wait_send()
        for d in range(1, 4):
            m_copy(j, d).wait_send()


def body(act_table, token_ids, lengths, grads, weights):
    n = len(CHUNKS)
    wide = sum(CHUNKS)
    dma = pltpu.SemaphoreType.DMA
    whole = pl.BlockSpec(memory_space=pltpu.VMEM)
    anywhere = pl.BlockSpec(memory_space=pl.ANY)
    return pl.pallas_call(
        kernel,
        out_shape=(
            jax.ShapeDtypeStruct((1, 256, wide), jnp.bfloat16),
            jax.ShapeDtypeStruct((1, 256, wide), jnp.float32),
        ),
        in_specs=[anywhere, whole, pl.BlockSpec(memory_space=pltpu.SMEM), anywhere, anywhere],
        out_specs=(whole, whole),
        scratch_shapes=[
            pltpu.VMEM((2048, 128), jnp.bfloat16),
            pltpu.VMEM((128, 2048), jnp.bfloat16),
            tuple(pltpu.VMEM((16, 128, 128), jnp.bfloat16) for _ in range(8)),
            pltpu.VMEM((8, 1024, 512), jnp.bfloat16),
            pltpu.VMEM((8, 512, max(CHUNKS)), jnp.bfloat16),
            pltpu.VMEM((256, max(CHUNKS)), jnp.float32),
            pltpu.VMEM((256, wide), jnp.bfloat16),
            pltpu.VMEM((3, 256, wide), jnp.bfloat16),
            pltpu.VMEM((256, wide), jnp.float32),
            tuple(pltpu.VMEM((1024, w), jnp.int16) for w in CHUNKS),
            tuple(pltpu.VMEM((3, 256, w), jnp.int16) for w in CHUNKS),
            tuple(pltpu.VMEM((16, 128, w), jnp.bfloat16) for w in CHUNKS),
            dma, dma, dma((8,)), dma((8,)), dma((n,)), dma((n,)), dma((n, 4)), dma((n, 4)),
            dma((3,)), dma((3,)), dma((n, 3)), dma((n, 3)), dma,
        ],
        compiler_params=pltpu.CompilerParams(
            collective_id=0, has_side_effects=True, vmem_limit_bytes=50 << 20
        ),
    )(act_table, token_ids, lengths, grads, weights)


def solution(mesh):
    placed = (
        P("ckpt", "fsdp", None),
        P("ckpt", None),
        P("ckpt", None),
        P("ckpt", "fsdp", None),
        P("ckpt", "fsdp", None, None),
    )
    return jax.shard_map(
        body,
        mesh=mesh,
        in_specs=placed,
        out_specs=(P("fsdp", "ckpt", None), P("fsdp", "ckpt", None)),
        check_vma=False,
    )
```

time: 121 us -> 104 us (0.86)
  Pallas kernels: 116 us -> 98.8 us
    pallas_call x1, Pallas kernels: 116 us -> 98.8 us  [body(): pl.pallas_call(kernel, out_shape=(jax.ShapeDtypeStruct((1, 256, wide), jn...]
    unnamed x4 -> x8, local copies, waits for them, and re-layouts: 3.53 us -> 4.54 us
where the time goes in v2:
time: 104 us
  Pallas kernels  98.8 us (95%)
  local copies, waits for them, and re-layouts  4.54 us (4%)
    pallas_call x1, Pallas kernels, body(): pl.pallas_call(kernel, out_shape=(jax.ShapeDtypeStruct((1, 256, wide), jn...  98.8 us
    unnamed x8, local copies, waits for them, and re-layouts  4.54 us

profile of v2, /device:TPU:1, one launch (start us, length us, event | category | flops | bytes accessed | tf_op | source)
XLA Modules:
  0.0 103.9 jit_solution(1466091607243589638)
XLA Ops:
  0.6 0.0 copy-start
  0.6 1.0 copy-done
  1.7 0.0 copy-start.1
  1.7 0.7 copy-done.1
  2.4 0.0 copy-start.2
  2.4 0.7 copy-done.2
  3.0 98.8 %shard_map.68 = (bf16[1,256,1792]{2,1,0:T(8,128)(2,1)S(1)}, f32[1,256,1792]{2,1,0:T(8,128)S(1)}) custom-call(bf16[1,64,4096]{2,1,0:T(8,128)(2,1)S(1)} %copy-done, s32[1,2048]{1,0:T(1,128)S(1)} %copy-done.1, s32[1,8]{1,0:T(1,128)S(1)} %copy-done.2, bf16[1,64,14336]{2,1,0:T(8,128)(2,1)} %grads.1, bf16[1,1,1024,1792]{3,2,1,0:T(8,128)(2,1)} %weights.1), custom_call_target="tpu_custom_call" | custom-call | tf_op jit(solution)/shard_map/pallas_call | solution.py:329
  101.8 0.9 copy.9
  102.7 1.2 %copy.10 = f32[1,256,1792]{2,1,0:T(8,128)} copy(f32[1,256,1792]{2,1,0:T(8,128)S(1)} %get-tuple-element.5) | data formatting | bytes 3670016
Async XLA Ops:
  0.6 1.0 %copy-start = (bf16[1,64,4096]{2,1,0:T(8,128)(2,1)S(1)}, bf16[1,64,4096]{2,1,0:T(8,128)(2,1)}, u32[]{:S(2)}) copy-start(bf16[1,64,4096]{2,1,0:T(8,128)(2,1)} %act.1) | copy-start | bytes 1572868
  1.7 0.7 copy-start.1
  2.4 0.7 copy-start.2

commit v3 on v2

--- a/solution.py
+++ b/solution.py
@@ -326,6 +326,8 @@
     dma = pltpu.SemaphoreType.DMA
     whole = pl.BlockSpec(memory_space=pltpu.VMEM)
     anywhere = pl.BlockSpec(memory_space=pl.ANY)
+    operands = (act_table, token_ids, lengths, grads, weights)
+    operands = [pltpu.with_memory_space_constraint(operand, pltpu.HBM) for operand in operands]
     return pl.pallas_call(
         kernel,
         out_shape=(
@@ -353,7 +355,7 @@
         compiler_params=pltpu.CompilerParams(
             collective_id=0, has_side_effects=True, vmem_limit_bytes=50 << 20
         ),
-    )(act_table, token_ids, lengths, grads, weights)
+    )(*operands)
 
 
 def solution(mesh):

time: 104 us -> 102 us (0.981)
  local copies, waits for them, and re-layouts: 4.54 us -> 2.15 us
    unnamed x8 -> x2, local copies, waits for them, and re-layouts: 4.54 us -> 2.15 us
where the time goes in v3:
time: 102 us
  Pallas kernels  99.3 us (97%)
  local copies, waits for them, and re-layouts  2.15 us (2%)
    pallas_call x1, Pallas kernels, body(): pl.pallas_call(kernel, out_shape=(jax.ShapeDtypeStruct((1, 256, wide), jn...  99.3 us
    unnamed x2, local copies, waits for them, and re-layouts  2.15 us

profile of v3, /device:TPU:1, one launch (start us, length us, event | category | flops | bytes accessed | tf_op | source)
XLA Modules:
  0.0 102.1 jit_solution(262914683652993548)
XLA Ops:
  0.6 99.3 %shard_map.68 = (bf16[1,256,1792]{2,1,0:T(8,128)(2,1)S(1)}, f32[1,256,1792]{2,1,0:T(8,128)S(1)}) custom-call(bf16[1,64,4096]{2,1,0:T(8,128)(2,1)} %act.1, s32[1,2048]{1,0:T(1,128)} %ids.1, s32[1,8]{1,0:T(1,128)} %lengths.1, bf16[1,64,14336]{2,1,0:T(8,128)(2,1)} %grads.1, bf16[1,1,1024,1792]{3,2,1,0:T(8,128)(2,1)} %weights.1), custom_call_target="tpu_custom_call" | custom-call | tf_op jit(solution)/shard_map/pallas_call | solution.py:331
  99.9 0.9 copy.9
  100.8 1.2 %copy.10 = f32[1,256,1792]{2,1,0:T(8,128)} copy(f32[1,256,1792]{2,1,0:T(8,128)S(1)} %get-tuple-element.5) | data formatting | bytes 3670016

commit v4 on v3

--- a/solution.py
+++ b/solution.py
@@ -12,7 +12,7 @@
 SCALE = 65535.0 / (HIGH - LOW)
 MESH = pl.DeviceIdType.MESH
 ORDER = (
-    "A", "z0", "W", "z1", "H", "z2", "s0", "s1", "T", "P", "G", "z3", "s2", "p0", "X", "B", "U", "z4",
+    "A", "z0", "W", "z1", "H", "z2", "s0", "s1", "T", "P0", "g", "P1", "G", "z3", "s2", "p0", "X", "B", "U", "z4",
     "s3", "p1", "F", "z5", "Y", "Z", "s4", "p2", "z6", "z7", "f0", "c0", "p3", "s5", "f1", "c1", "p4",
     "s6", "f2", "c2", "V", "o0", "p5", "s7", "f3", "c3", "o1", "p6", "f4", "c4", "o2", "p7", "f5", "c5",
     "o3", "f6", "c6", "o4", "f7", "c7", "o5", "o6", "o7",
@@ -160,8 +160,8 @@
                 hot = jnp.where(hot, jnp.float32(1), jnp.float32(0)).astype(jnp.bfloat16)
                 windows[b, :, h * 256 : (h + 1) * 256] = hot
 
-    def a_permute():
-        @pl.loop(0, 8)
+    def a_permute(half):
+        @pl.loop(half * 4, half * 4 + 4)
         def _(b):
             placed = sum(
                 jnp.dot(
@@ -180,21 +180,24 @@
 
     def g_copy(i):
         src, dst, target = (
-            (act_t[0], act_t[1], above_core),
-            (act_t[0], act_t[2], below_core),
+            (act_t[0].at[first_half], act_t[1].at[first_half], above_core),
+            (act_t[0].at[second_half], act_t[2].at[second_half], below_core),
             (act_t[1].at[first_half], act_t[3].at[first_half], above_core),
             (act_t[2].at[second_half], act_t[3].at[second_half], below_core),
             (act_t[0], act_t[4], other_core),
             (act_t[1], act_t[5], other_core),
             (act_t[2], act_t[6], other_core),
             (act_t[3], act_t[7], other_core),
+            (act_t[0].at[second_half], act_t[1].at[second_half], above_core),
+            (act_t[0].at[first_half], act_t[2].at[first_half], below_core),
         )[i]
         return remote(src, dst, g_send.at[i], g_recv.at[i], target)
 
     def g_arrived(i):
         part = (
-            act_t[1], act_t[2], act_t[3].at[first_half], act_t[3].at[second_half],
+            act_t[1].at[first_half], act_t[2].at[second_half], act_t[3].at[first_half], act_t[3].at[second_half],
             act_t[4], act_t[5], act_t[6], act_t[7],
+            act_t[1].at[second_half], act_t[2].at[first_half],
         )[i]
         sized(part, g_recv.at[i])
 
@@ -207,17 +210,23 @@
                 windows[e, rows, at] = act_t[k][lead[e] + i] * keeps[e][:, at]
 
     def g_start():
-        for i in (0, 1, 4):
+        for i in (1, 8, 4):
+            g_copy(i).start()
+
+    def g_start_half():
+        for i in (0, 9):
             g_copy(i).start()
 
     def g_below():
         g_arrived(0)
         g_copy(2).start()
+        g_arrived(8)
         g_copy(5).start()
 
     def g_above():
         g_arrived(1)
         g_copy(3).start()
+        g_arrived(9)
         g_copy(6).start()
 
     def g_far():
@@ -301,7 +310,7 @@
 
     steps = {
         "z": z_start, "s": x_start, "p": x_pass, "f": x_finish, "c": compute, "o": combine,
-        "A": a_start, "W": w_start, "V": w_arrived, "T": a_turn, "H": hot_build, "P": a_permute, "G": g_start, "B": g_below,
+        "A": a_start, "W": w_start, "V": w_arrived, "T": a_turn, "H": hot_build, "P": a_permute, "G": g_start, "g": g_start_half, "B": g_below,
         "U": g_above, "F": g_far, "X": mask_own, "Y": mask_near, "Z": mask_far,
     }
     for step in ORDER:
@@ -310,7 +319,7 @@
     pltpu.make_async_copy(piece.at[pl.ds(0, 31 * 64)], piece.at[pl.ds(0, 31 * 64)], a_send).wait()
     for copy in w_copies:
         copy.wait_send()
-    for i in range(8):
+    for i in range(10):
         g_copy(i).wait_send()
     for j in range(n):
         sized(blocks[j].at[pl.ds(0, 7), pl.ds(0, 64)], z_send.at[j])
@@ -349,7 +358,7 @@
             tuple(pltpu.VMEM((1024, w), jnp.int16) for w in CHUNKS),
             tuple(pltpu.VMEM((3, 256, w), jnp.int16) for w in CHUNKS),
             tuple(pltpu.VMEM((16, 128, w), jnp.bfloat16) for w in CHUNKS),
-            dma, dma, dma((8,)), dma((8,)), dma((n,)), dma((n,)), dma((n, 4)), dma((n, 4)),
+            dma, dma, dma((10,)), dma((10,)), dma((n,)), dma((n,)), dma((n, 4)), dma((n, 4)),
             dma((3,)), dma((3,)), dma((n, 3)), dma((n, 3)), dma,
         ],
         compiler_params=pltpu.CompilerParams(

time: 102 us -> 102 us (level)
  no operation moved by 1% of the time
where the time goes in v4:
time: 102 us
  Pallas kernels  98.8 us (97%)
  local copies, waits for them, and re-layouts  2.15 us (2%)
    pallas_call x1, Pallas kernels, body(): pl.pallas_call(kernel, out_shape=(jax.ShapeDtypeStruct((1, 256, wide), jn...  98.8 us
    unnamed x2, local copies, waits for them, and re-layouts  2.15 us

profile of v4, /device:TPU:1, one launch (start us, length us, event | category | flops | bytes accessed | tf_op | source)
XLA Modules:
  0.0 101.6 jit_solution(4696748371258200550)
XLA Ops:
  0.6 98.8 %shard_map.68 = (bf16[1,256,1792]{2,1,0:T(8,128)(2,1)S(1)}, f32[1,256,1792]{2,1,0:T(8,128)S(1)}) custom-call(bf16[1,64,4096]{2,1,0:T(8,128)(2,1)} %act.1, s32[1,2048]{1,0:T(1,128)} %ids.1, s32[1,8]{1,0:T(1,128)} %lengths.1, bf16[1,64,14336]{2,1,0:T(8,128)(2,1)} %grads.1, bf16[1,1,1024,1792]{3,2,1,0:T(8,128)(2,1)} %weights.1), custom_call_target="tpu_custom_call" | custom-call | tf_op jit(solution)/shard_map/pallas_call | solution.py:340
  99.4 0.9 copy.9
  100.4 1.2 %copy.10 = f32[1,256,1792]{2,1,0:T(8,128)} copy(f32[1,256,1792]{2,1,0:T(8,128)S(1)} %get-tuple-element.5) | data formatting | bytes 3670016

commit v5 on v4

--- a/solution.py
+++ b/solution.py
@@ -12,7 +12,7 @@
 SCALE = 65535.0 / (HIGH - LOW)
 MESH = pl.DeviceIdType.MESH
 ORDER = (
-    "A", "z0", "W", "z1", "H", "z2", "s0", "s1", "T", "P0", "g", "P1", "G", "z3", "s2", "p0", "X", "B", "U", "z4",
+    "A", "z0", "z1", "H", "W", "z2", "s0", "s1", "T", "P0", "g", "P1", "G", "z3", "s2", "p0", "X", "B", "U", "z4",
     "s3", "p1", "F", "z5", "Y", "Z", "s4", "p2", "z6", "z7", "f0", "c0", "p3", "s5", "f1", "c1", "p4",
     "s6", "f2", "c2", "V", "o0", "p5", "s7", "f3", "c3", "o1", "p6", "f4", "c4", "o2", "p7", "f5", "c5",
     "o3", "f6", "c6", "o4", "f7", "c7", "o5", "o6", "o7",

time: 102 us -> 102 us (level)
  no operation moved by 1% of the time
where the time goes in v5:
time: 102 us
  Pallas kernels  98.8 us (97%)
  local copies, waits for them, and re-layouts  2.15 us (2%)
    pallas_call x1, Pallas kernels, body(): pl.pallas_call(kernel, out_shape=(jax.ShapeDtypeStruct((1, 256, wide), jn...  98.8 us
    unnamed x2, local copies, waits for them, and re-layouts  2.15 us

profile of v5, /device:TPU:1, one launch (start us, length us, event | category | flops | bytes accessed | tf_op | source)
XLA Modules:
  0.0 101.6 jit_solution(167068573416687670)
XLA Ops:
  0.6 98.8 %shard_map.68 = (bf16[1,256,1792]{2,1,0:T(8,128)(2,1)S(1)}, f32[1,256,1792]{2,1,0:T(8,128)S(1)}) custom-call(bf16[1,64,4096]{2,1,0:T(8,128)(2,1)} %act.1, s32[1,2048]{1,0:T(1,128)} %ids.1, s32[1,8]{1,0:T(1,128)} %lengths.1, bf16[1,64,14336]{2,1,0:T(8,128)(2,1)} %grads.1, bf16[1,1,1024,1792]{3,2,1,0:T(8,128)(2,1)} %weights.1), custom_call_target="tpu_custom_call" | custom-call | tf_op jit(solution)/shard_map/pallas_call | solution.py:340
  99.4 0.9 copy.9
  100.4 1.2 %copy.10 = f32[1,256,1792]{2,1,0:T(8,128)} copy(f32[1,256,1792]{2,1,0:T(8,128)S(1)} %get-tuple-element.5) | data formatting | bytes 3670016
